TPU v7x, 32 devices: a whole 2x2x4 slice. The times are simulated.
32 devices in a mesh: ccd: 16 (over z, y, x), strip: 2 (over core).
Axes of the slice: x: 2, y: 2, z: 4, core: 2. Of those that a mesh axis runs over, the one named last changes fastest.
Arguments:
- coadd_blocks: bfloat16 [4096, 512], P(('ccd', 'strip')), may hold values from -10.5 to 10.5
- block_route: int32 [1024, 1], P(('ccd', 'strip')), may hold values from 0 to 31, as said below
- block_offset: int32 [1024], P(('ccd', 'strip')), may hold values from 0 to 380
- warp_matrix: bfloat16 [8192, 384], P(('ccd', 'strip')), may hold values from -0.1875 to 0.1875
- science: float32 [8192, 512], P(('ccd', 'strip')), may hold values from -6 to 6
- basis_columns: bfloat16 [21, 21], replicated, may hold values from -0.375 to 0.375
- basis_rows: bfloat16 [21, 21], replicated, may hold values from -0.375 to 0.375
- stamp_corner: int32 [256, 2], P(('ccd', 'strip')), may hold values from 0 to 480, as said below
- stamp_count: int32 [32], P(('ccd', 'strip')), may hold values from 1 to 8, as said below
- kernel_prior: float32 [132], replicated, may hold values from -4 to 4
Outputs:
- difference: float32 [8192, 512], P(('ccd', 'strip'))
- stamp_residuals: float32 [256, 1024], P(('ccd', 'strip'))
- kernel_solution: float32 [132], replicated
Inputs may be any that keep to these rules, and one draw needn't show every extreme that they name: `block_route`: among the 32 blocks of one device at most 2 name the same device, and in every draw some device is named exactly 2 times by the blocks of every device. `stamp_corner`: every stamp lies inside its strip (row corners at most 224, column corners at most 480), and the stamps of one device never intersect. `stamp_count`: some device has all 8 slots live.
All inputs are finite; a program needn't handle non-finite values.
Results may differ from a plain program's by a relative error of at most 0.002.
The roundings to bfloat16 on the way count: a program that leaves them out, or rounds other values in their place, can miss the bound.
Values may be sent and summed in bfloat16 or wider, within the bound.
A program may use at most 128 MiB of HBM per device.

v0:
```python
import jax
import jax.numpy as jnp
from jax import lax
from jax.sharding import PartitionSpec as P

CAP = 2
SS = 32


def extended(array, sides, width):
    for axis, dim in sides:
        size, length = (lax.axis_size(axis), array.shape[dim])
        up = [(i, (i + 1) % size) for i in range(size - 1)]
        down = [(j, i) for i, j in up]
        last = lax.slice_in_dim(array, length - width, length, axis=dim)
        initial = lax.slice_in_dim(array, 0, width, axis=dim)
        before = lax.ppermute(last, axis, up)
        after = lax.ppermute(initial, axis, down)
        array = jnp.concatenate([before, array, after], axis=dim)
    return array


def band_table(kernel_taps, height, outputs):
    lagging = (
        jnp.arange(height, dtype=jnp.int32)[:, None] - jnp.arange(outputs, dtype=jnp.int32)[None, :]
    )
    selector = (
        lagging[:, :, None] == jnp.arange(kernel_taps.shape[1], dtype=jnp.int32)[None, None, :]
    ).astype(jnp.bfloat16)
    return jnp.einsum(
        "kj,woj->kwo", kernel_taps, selector, preferred_element_type=jnp.float32
    ).astype(jnp.bfloat16)


def legendre_terms(yvalue, xvalue):
    filler = jnp.zeros_like(yvalue + xvalue)
    return jnp.stack(
        [
            filler + 1.0,
            filler + xvalue,
            filler + yvalue,
            filler + 1.5 * xvalue * xvalue - 0.5,
            xvalue * yvalue,
            filler + 1.5 * yvalue * yvalue - 0.5,
        ]
    )


def polynomial_sum(coefficient, yvalue, xvalue):
    return (
        coefficient[0]
        + coefficient[1] * xvalue
        + coefficient[2] * yvalue
        + coefficient[3] * (1.5 * xvalue * xvalue - 0.5)
        + coefficient[4] * (xvalue * yvalue)
        + coefficient[5] * (1.5 * yvalue * yvalue - 0.5)
    )


def feature_rows(convolved, polynomials):
    products = (convolved.astype(jnp.float32)[:, None, :] * polynomials[None, :, :]).astype(
        jnp.bfloat16
    )
    return jnp.concatenate(
        [products.reshape(-1, polynomials.shape[1]), polynomials.astype(jnp.bfloat16)], axis=0
    )


def fit_terms(features, weights, targets):
    weighted = features * weights.astype(jnp.bfloat16)[None, :]
    normal_matrix = lax.dot_general(
        weighted, features, (((1,), (1,)), ((), ())), preferred_element_type=jnp.float32
    )
    right_side = jnp.dot(
        features.astype(jnp.float32), weights * targets, precision=lax.Precision.HIGHEST
    )
    return (normal_matrix, right_side)


def spd_solve(system, wanted):
    order = system.shape[0]
    position = jnp.arange(order, dtype=jnp.int32)

    def eliminate(step, carry):
        matrix, vector = carry
        marker = (position == step).astype(matrix.dtype)
        pivot_row = jnp.sum(matrix * marker[:, None], axis=0)
        pivot_column = jnp.sum(matrix * marker[None, :], axis=1)
        pivot = jnp.sum(pivot_row * marker)
        pivot_value = jnp.sum(vector * marker)
        factor = pivot_column / pivot * (1.0 - marker)
        return (matrix - factor[:, None] * pivot_row[None, :], vector - factor * pivot_value)

    matrix, vector = lax.fori_loop(0, order, eliminate, (system, wanted))
    diagonal = jnp.sum(matrix * jnp.eye(order, dtype=matrix.dtype), axis=1)
    return vector / diagonal


def global_fit(normal_matrix, right_side, pixels, kernel_prior):
    normal_matrix, right_side, pixels = lax.psum(
        (normal_matrix, right_side, pixels), ("ccd", "strip")
    )
    system = normal_matrix / pixels + jnp.eye(normal_matrix.shape[0], dtype=jnp.float32)
    wanted = right_side / pixels + kernel_prior
    return spd_solve(system, wanted)


def cut_windows(image_field, corner_rows, corner_columns, height, width):
    slot_total = corner_rows.shape[0]
    leading = image_field.shape[:-2]
    lead_zeros = tuple((jnp.zeros((), jnp.int32) for axis_number in leading))
    stacked = jnp.zeros((slot_total,) + leading + (height, width), image_field.dtype)

    def place(slot, holder):
        row_start = lax.dynamic_index_in_dim(corner_rows, slot, keepdims=False)
        column_start = lax.dynamic_index_in_dim(corner_columns, slot, keepdims=False)
        piece = lax.dynamic_slice(
            image_field, lead_zeros + (row_start, column_start), leading + (height, width)
        )
        anchor = (slot,) + lead_zeros + (jnp.zeros((), jnp.int32), jnp.zeros((), jnp.int32))
        return lax.dynamic_update_slice(holder, piece[None], anchor)

    return lax.fori_loop(0, slot_total, place, stacked)


def full_convolution(widened, basis_columns, basis_rows, strip_rows, strip_width):
    half_width = basis_columns.shape[1] // 2
    tile_width = min(128, strip_width)
    windows = jnp.stack(
        [
            widened[
                :, tile_index * tile_width : tile_index * tile_width + tile_width + 2 * half_width
            ]
            for tile_index in range(strip_width // tile_width)
        ]
    )
    across = band_table(basis_columns, tile_width + 2 * half_width, tile_width)
    column_pass = jnp.einsum(
        "trw,kwo->krto", windows, across, preferred_element_type=jnp.float32
    ).astype(jnp.bfloat16)
    column_pass = column_pass.reshape(column_pass.shape[0], column_pass.shape[1], strip_width)
    downward = band_table(basis_rows, strip_rows + 2 * half_width, strip_rows)
    return jnp.einsum(
        "kio,kic->koc", downward, column_pass, preferred_element_type=jnp.float32
    ).astype(jnp.bfloat16)


def masked_terms(convolved, polynomials, science, corner_rows, corner_columns, live_slot):
    strip_rows = science.shape[0]
    strip_width = science.shape[1]
    row_index = jnp.arange(strip_rows, dtype=jnp.int32)[None, :]
    column_index = jnp.arange(strip_width, dtype=jnp.int32)[None, :]
    inside_rows = (
        live_slot[:, None]
        & (row_index >= corner_rows[:, None])
        & (row_index < corner_rows[:, None] + SS)
    )
    inside_columns = (column_index >= corner_columns[:, None]) & (
        column_index < corner_columns[:, None] + SS
    )
    coverage = jnp.dot(
        inside_rows.astype(jnp.bfloat16).T,
        inside_columns.astype(jnp.bfloat16),
        preferred_element_type=jnp.float32,
    )
    kernels = convolved.shape[0]
    unknowns = kernels * 6 + 6
    band_rows = 8

    def accumulate(band_index, partial_value):
        band_start = band_index * band_rows
        conv_band = lax.dynamic_slice_in_dim(convolved, band_start, band_rows, 1).reshape(
            kernels, -1
        )
        poly_band = lax.dynamic_slice_in_dim(polynomials, band_start, band_rows, 1).reshape(6, -1)
        weight_band = lax.dynamic_slice_in_dim(coverage, band_start, band_rows, 0).reshape(-1)
        target_band = lax.dynamic_slice_in_dim(science, band_start, band_rows, 0).reshape(-1)
        normal_part, right_part = fit_terms(
            feature_rows(conv_band, poly_band), weight_band, target_band
        )
        return (partial_value[0] + normal_part, partial_value[1] + right_part)

    zero_sums = (jnp.zeros((unknowns, unknowns), jnp.float32), jnp.zeros((unknowns,), jnp.float32))
    return lax.fori_loop(0, strip_rows // band_rows, accumulate, zero_sums)


def local(
    coadd_blocks,
    block_route,
    block_offset,
    warp_matrix,
    science,
    basis_columns,
    basis_rows,
    stamp_corner,
    stamp_count,
    kernel_prior,
):
    ccd_count = lax.axis_size("ccd")
    strip_count = lax.axis_size("strip")
    device_total = ccd_count * strip_count
    device_index = lax.axis_index("ccd") * strip_count + lax.axis_index("strip")
    block_total = block_offset.shape[0]
    block_rows = coadd_blocks.shape[0] // block_total
    strip_rows = science.shape[0]
    strip_width = science.shape[1]
    frame_height = warp_matrix.shape[1]
    destination = block_route[:, 0]
    matching = destination[:, None] == destination[None, :]
    earlier = (
        jnp.arange(block_total, dtype=jnp.int32)[:, None]
        > jnp.arange(block_total, dtype=jnp.int32)[None, :]
    )
    ranking = jnp.sum((matching & earlier).astype(jnp.int32), axis=1)
    slot_index = destination * CAP + ranking
    selection = jnp.arange(device_total * CAP, dtype=jnp.int32)[:, None] == slot_index[None, :]
    outgoing = jnp.dot(
        selection.astype(jnp.bfloat16),
        coadd_blocks.reshape(block_total, block_rows * strip_width),
        preferred_element_type=jnp.float32,
    ).astype(jnp.bfloat16)
    outgoing = outgoing.reshape(ccd_count, strip_count, CAP, block_rows, strip_width)
    landing = jnp.sum(jnp.where(selection, block_offset[None, :], 0), axis=1).reshape(
        ccd_count, strip_count, CAP
    )
    arrived, landed = (
        lax.all_to_all(
            lax.all_to_all(outgoing, "ccd", split_axis=0, concat_axis=0, tiled=True),
            "strip",
            split_axis=1,
            concat_axis=1,
            tiled=True,
        ),
        lax.all_to_all(
            lax.all_to_all(landing, "ccd", split_axis=0, concat_axis=0, tiled=True),
            "strip",
            split_axis=1,
            concat_axis=1,
            tiled=True,
        ),
    )
    placed_rows = (
        landed.reshape(-1, 1) + jnp.arange(block_rows, dtype=jnp.int32)[None, :]
    ).reshape(-1)
    placement = (jnp.arange(frame_height, dtype=jnp.int32)[:, None] == placed_rows[None, :]).astype(
        jnp.bfloat16
    )
    source_frame = jnp.dot(
        placement, arrived.reshape(-1, strip_width), preferred_element_type=jnp.float32
    ).astype(jnp.bfloat16)
    template = jnp.dot(warp_matrix, source_frame, preferred_element_type=jnp.float32).astype(
        jnp.bfloat16
    )
    half_width = basis_columns.shape[1] // 2
    padded = extended(template, ((("ccd", "strip"), 0),), half_width)
    widened = jnp.pad(padded, ((0, 0), (half_width, half_width)))
    corner_rows = stamp_corner[:, 0]
    corner_columns = stamp_corner[:, 1]
    live_slot = jnp.arange(stamp_corner.shape[0], dtype=jnp.int32) < stamp_count[0]
    local_pixels = stamp_count[0].astype(jnp.float32) * (SS * SS)
    first_row = device_index * strip_rows
    total_rows = device_total * strip_rows
    convolved = full_convolution(widened, basis_columns, basis_rows, strip_rows, strip_width)
    row_coord = (
        (2 * (first_row + jnp.arange(strip_rows, dtype=jnp.int32)) + 1).astype(jnp.float32)
        / total_rows
        - 1.0
    )[:, None]
    column_coord = (
        (2 * jnp.arange(strip_width, dtype=jnp.int32) + 1).astype(jnp.float32) / strip_width - 1.0
    )[None, :]
    polynomials = legendre_terms(row_coord, column_coord)
    normal_matrix, right_side = masked_terms(
        convolved, polynomials, science, corner_rows, corner_columns, live_slot
    )
    solution = global_fit(normal_matrix, right_side, local_pixels, kernel_prior)
    kernels = basis_columns.shape[0]
    coefficient = solution[: kernels * 6].reshape(kernels, 6).T[:, :, None, None]
    weight_fields = polynomial_sum(coefficient, row_coord[None], column_coord[None])
    background = polynomial_sum(solution[kernels * 6 :], row_coord, column_coord)
    matched = jnp.sum(convolved.astype(jnp.float32) * weight_fields, axis=0) + background
    difference = science - matched
    residuals = (
        cut_windows(difference, corner_rows, corner_columns, SS, SS)
        * live_slot.astype(jnp.float32)[:, None, None]
    )
    return (difference, residuals.reshape(residuals.shape[0], SS * SS), solution)


def solution(mesh):
    in_specs = (
        P(("ccd", "strip"), None),
        P(("ccd", "strip"), None),
        P(("ccd", "strip")),
        P(("ccd", "strip"), None),
        P(("ccd", "strip"), None),
        P(),
        P(),
        P(("ccd", "strip"), None),
        P(("ccd", "strip")),
        P(),
    )
    out_specs = (P(("ccd", "strip"), None), P(("ccd", "strip"), None), P())
    return jax.shard_map(local, mesh=mesh, in_specs=in_specs, out_specs=out_specs, check_vma=False)
```

profile of v0, /device:TPU:0, one launch (start us, length us, event | category | flops | bytes accessed | tf_op | source)
XLA Modules:
  0.0 792.5 jit_solution(13051606889551345449)
XLA Ops:
  10.3 8.3 %all-to-all-start = ((s32[16,2,2]{2,1,0:T(2,128)}), s32[16,2,2]{2,1,0:T(2,128)S(1)}, u32[]{:S(2)}, u32[]{:S(2)}) async-start(s32[16,2,2]{2,1,0:T(2,128)} %reshape.485), calls=%async_computation | async-start | bytes 32768 | tf_op jit(solution)/shard_map/all_to_all | solution.py:235
  25.1 3.4 convert_bitcast_fusion.1
  31.5 3.7 all_to_all.20
  35.2 6.9 all-to-all-start.2
  43.2 9.1 %all-to-all-done.2 = bf16[16,2,2,4,512]{4,3,2,1,0:T(4,128)(2,1)S(1)} async-done(((bf16[16,2,2,4,512]{4,3,2,1,0:T(4,128)(2,1)}), bf16[16,2,2,4,512]{4,3,2,1,0:T(4,128)(2,1)S(1)}, u32[]{:S(2)}, u32[]{:S(2)}) %all-to-all-start.2) | async-done | bytes 262176 | tf_op jit(solution)/shard_map/all_to_all | solution.py:228
  52.4 3.9 all_to_all.21
  57.1 2.1 collective-permute-start
  59.1 1.5 collective-permute-start.1
  61.1 1.3 collective-permute-done.1
  62.8 1.8 convert_bitcast_fusion
  64.6 4.9 copy.45
  69.4 10.5 %reshape.489 = bf16[21,276,512]{2,1,0:T(8,128)(2,1)} reshape(bf16[21,276,4,128]{3,2,1,0:T(4,128)(2,1)} %copy.45) | data formatting | bytes 11870208 | tf_op jit(solution)/shard_map/reshape | solution.py:141
  79.9 9.3 %convolution_convert_fusion = bf16[21,256,512]{2,1,0:T(8,128)(2,1)} fusion(bf16[21,276,512]{2,1,0:T(8,128)(2,1)} %reshape.489, bf16[21,276,256]{2,0,1:T(8,128)(2,1)} %convert_bitcast_fusion.1), kind=kOutput, calls=%fused_computation.34 | convolution fusion | flops 1522139136 | bytes 14407680 | tf_op jit(solution)/shard_map/kio,kic->koc/dot_general | solution.py:143
  89.2 226.9 %while.47 = (s32[]{:T(128)}, f32[132,132]{1,0:T(8,128)S(1)}, f32[132]{0:T(256)}, bf16[21,256,512]{2,1,0:T(8,128)(2,1)}, f32[6,256,512]{2,1,0:T(8,128)}, /*index=...) while((s32[]{:T(128)}, f32[132,132]{1,0:T(8,128)S(1)}, ...), condition=%wide.region_3.4_spmd.clone, body=%wide.region_2.3_spmd.clone.sunk | while | flops 157976864 | bytes 8563074 | solution.py:184
  316.8 42.9 %all-reduce.1 = (f32[]{:T(128)}, f32[132]{0:T(256)S(1)}) all-reduce(f32[]{:T(128)S(6)} %mul.572, f32[132]{0:T(256)} %get-tuple-element.303), channel_id=1, replica_groups=mesh['ccd'=16,'strip'=2] {'ccd','strip'}, use_global_device_ids=true, to_apply=%region_5.6 | all-reduce | flops 133 | bytes 1064 | tf_op jit(solution)/shard_map/psum | solution.py:100
  359.7 1.4 divide_add_fusion
  361.1 79.3 %all-reduce.4.cloned.1.call-done = f32[132,132]{1,0:T(8,128)} async-done(((f32[132,132]{1,0:T(8,128)}), f32[132,132]{1,0:T(8,128)}) %all-reduce.4.cloned.1.call-update) | async-done | bytes 69712 | tf_op jit(solution)/shard_map/psum | solution.py:100
  440.4 1.6 convert_add_fusion
  442.0 289.2 %while.46 = (s32[]{:T(128)}, f32[132,132]{1,0:T(8,128)S(1)}, f32[132]{0:T(256)S(1)}, s32[]{:T(128)}) while((s32[]{:T(128)}, f32[132,132]{1,0:T(8,128)S(1)}, f32[132]{0:T(256)S(1)}, s32[]{:T(128)}) %tuple.115), condition=%wide.region_12.13_spmd.clone, body=%wide.region_7.12_spmd.clone.sunk | while | flops 106128 | bytes 215505 | solution.py:94
  447.1 1.3 multiply_subtract_fusion.4
  451.5 1.3 multiply_subtract_fusion.4
  453.7 1.3 multiply_subtract_fusion.4
  458.1 1.3 multiply_subtract_fusion.4
  464.7 1.3 multiply_subtract_fusion.4
  471.2 1.3 multiply_subtract_fusion.4
  475.6 1.3 multiply_subtract_fusion.4
  477.8 1.3 multiply_subtract_fusion.4
  482.2 1.3 multiply_subtract_fusion.4
  488.8 1.3 multiply_subtract_fusion.4
  493.2 1.3 multiply_subtract_fusion.4
  495.3 1.3 multiply_subtract_fusion.4
  499.7 1.3 multiply_subtract_fusion.4
  506.3 1.3 multiply_subtract_fusion.4
  512.9 1.3 multiply_subtract_fusion.4
  517.3 1.3 multiply_subtract_fusion.4
  519.4 1.3 multiply_subtract_fusion.4
  523.8 1.3 multiply_subtract_fusion.4
  530.4 1.3 multiply_subtract_fusion.4
  534.8 1.3 multiply_subtract_fusion.4
  537.0 1.3 multiply_subtract_fusion.4
  541.4 1.3 multiply_subtract_fusion.4
  547.9 1.3 multiply_subtract_fusion.4
  554.5 1.3 multiply_subtract_fusion.4
  558.9 1.3 multiply_subtract_fusion.4
  561.1 1.3 multiply_subtract_fusion.4
  565.5 1.3 multiply_subtract_fusion.4
  737.2 5.4 multiply_reduce_fusion.2
  743.6 41.2 %while.45 = (s32[]{:T(128)}, f32[8,32,32]{2,1,0:T(8,128)S(1)}, s32[8]{0:T(128)S(1)}, s32[8]{0:T(128)S(1)}, f32[256,512]{1,0:T(8,128)S(1)}, /*index=5*/s32[]{:T(128)}, s32[]{:T(128)}, s32[]{:T(128)}, s32[]{:T(128)}) while((s32[]{:T(128)}, f32[8,32,32]{2,1,0:T(8,128)S(1)}, s32[8]{0:T(128)S(1)}, s32[8]{0:T(128)S(1)}, ...), condition=%wide.region_16.17_spmd, body=%wide.region_15.16_spmd.sunk | while | flops 8 | bytes 32965 | solution.py:123
  (1227 shorter events, 506.9 us)
Async XLA Ops:
  7.2 49.4 %copy-start = (bf16[256,384]{1,0:T(8,128)(2,1)S(1)}, bf16[256,384]{1,0:T(8,128)(2,1)}, u32[]{:S(2)}) copy-start(bf16[256,384]{1,0:T(8,128)(2,1)} %param.19) | copy-start | bytes 589828
  7.2 17.2 %copy-start.13 = (s32[8,2]{0,1:T(2,128)S(1)}, s32[8,2]{0,1:T(2,128)}, u32[]{:S(2)}) copy-start(s32[8,2]{0,1:T(2,128)} %param.23) | copy-start | bytes 196
  7.2 17.9 %copy-start.8 = (bf16[21,21]{1,0:T(8,128)(2,1)S(1)}, bf16[21,21]{1,0:T(8,128)(2,1)}, u32[]{:S(2)}) copy-start(bf16[21,21]{1,0:T(8,128)(2,1)} %param.22) | copy-start | bytes 2650
  10.3 21.1 %all-to-all-start = ((s32[16,2,2]{2,1,0:T(2,128)}), s32[16,2,2]{2,1,0:T(2,128)S(1)}, u32[]{:S(2)}, u32[]{:S(2)}) async-start(s32[16,2,2]{2,1,0:T(2,128)} %reshape.485), calls=%async_computation | async-start | bytes 32768 | tf_op jit(solution)/shard_map/all_to_all | solution.py:235
  19.5 9.0 %copy-start.4 = (f32[512]{0:T(512)}, f32[512]{0:T(512)S(1)}, u32[]{:S(2)}) copy-start(f32[512]{0:T(512)S(1)} %fusion.53) | copy-start | bytes 6148
  20.9 8.5 %copy-start.6 = (f32[256]{0:T(256)}, f32[256]{0:T(256)S(1)}, u32[]{:S(2)}) copy-start(f32[256]{0:T(256)S(1)} %get-tuple-element.399) | copy-start | bytes 3076
  23.5 18.6 %copy-start.7 = (bf16[21,21]{1,0:T(8,128)(2,1)S(1)}, bf16[21,21]{1,0:T(8,128)(2,1)}, u32[]{:S(2)}) copy-start(bf16[21,21]{1,0:T(8,128)(2,1)} %param.21) | copy-start | bytes 2650
  24.4 18.2 %copy-start.9 = (s32[8]{0:T(128)}, s32[8]{0:T(128)S(1)}, u32[]{:S(2)}) copy-start(s32[8]{0:T(128)S(1)} %get-tuple-element.556) | copy-start | bytes 100
  24.4 18.2 %copy-start.11 = (s32[8]{0:T(128)}, s32[8]{0:T(128)S(1)}, u32[]{:S(2)}) copy-start(s32[8]{0:T(128)S(1)} %get-tuple-element.557) | copy-start | bytes 100
  35.2 17.1 %all-to-all-start.2 = ((bf16[16,2,2,4,512]{4,3,2,1,0:T(4,128)(2,1)}), bf16[16,2,2,4,512]{4,3,2,1,0:T(4,128)(2,1)S(1)}, u32[]{:S(2)}, u32[]{:S(2)}) async-start(bf16[16,2,2,4,512]{4,3,2,1,0:T(4,128)(2,1)} %reshape.487), calls=%async_computation.2 | async-start | bytes 524288 | tf_op jit(solution)/shard_map/all_to_all | solution.py:228
  42.1 398.3 %all-reduce.4.cloned.1.call-start = ((), (), s32[]{:S(2)}) async-start(), calls=%async_computation.4 | async-start | bytes 278528 | tf_op jit(solution)/shard_map/psum | solution.py:100
  57.1 4.1 collective-permute-start
  59.1 3.3 collective-permute-start.1
  316.2 0.7 copy-start.3
  731.3 11.3 %copy-start.5 = (f32[132]{0:T(256)}, f32[132]{0:T(256)S(1)}, u32[]{:S(2)}) copy-start(f32[132]{0:T(256)S(1)} %div.69) | copy-start | bytes 1588
  737.2 5.5 copy-start.1
  737.2 6.4 copy-start.10
  737.2 6.4 copy-start.12
  737.2 47.6 %copy-start.14 = (f32[8]{0:T(128)S(1)}, f32[8]{0:T(128)}, u32[]{:S(2)}) copy-start(f32[8]{0:T(128)} %fusion.56) | copy-start | bytes 100
  784.8 0.8 copy-start.2
Sparse Core Ops, SparseCore 0:
  317.0 123.3 all-reduce.3
where the time goes:
time: 807 us; the launch traced here: 792 us
  other arithmetic  404 us (50%)
  local copies, waits for them, and re-layouts  110 us (14%)
  waiting for transfers between devices  89.8 us (11%)
  matrix products  66.7 us (8%)
  blocking collectives  50.5 us (6%)
  loops' own time  38.1 us (5%)
  starting transfers between devices  18.8 us (2%)
  between operations  15.1 us (2%)
    sub x132, other arithmetic, eliminate(): vector - factor * pivot_value  172 us
    reduce_sum x132, other arithmetic, eliminate(): pivot = jnp.sum(pivot_row * marker)  80.2 us
    psum x1, waiting for transfers between devices, global_fit(): lax.psum((normal_matrix, right_side, pixels), ('ccd', 'strip'))  79.3 us
    while x224, local copies, waits for them, and re-layouts  63.3 us
    psum x1, blocking collectives, global_fit(): lax.psum((normal_matrix, right_side, pixels), ('ccd', 'strip'))  42.9 us
    add x32, other arithmetic, accumulate(): return (partial_value[0] + normal_part, partial_value[1] + right_part)  39.7 us
    another operation x1, loops' own time, cut_windows(): return lax.fori_loop(0, slot_total, place, stacked)  31.1 us
    dot_general x32, matrix products, fit_terms(): jnp.dot(features.astype(jnp.float32), weights * targets, precision=lax.Pr...  30.8 us
  transfers between devices with their start and end apart: 5, of which 3 were waited for; matrix products, arithmetic and copies ran while one was open for 2% of the time, Pallas kernels for 0%

commit v1 on v0

v1 whole, which is shorter than its diff:
```python
import functools

import jax
import jax.numpy as jnp
from jax import lax
from jax.experimental import pallas as pl
from jax.experimental.pallas import tpu as pltpu
from jax.sharding import PartitionSpec as P

SS = 32
NK = 21
KP = 24
NF = 6 * KP
NG = NF + 16
LP = 64
RP = 16
NT = (((1,), (1,)), ((), ()))
F32 = jnp.float32
BF16 = jnp.bfloat16


def iota(shape, dim):
    return lax.broadcasted_iota(jnp.int32, shape, dim)


def toeplitz(taps_ref, k):
    row = taps_ref[pl.ds(k, 1), :]
    return pltpu.roll(jnp.broadcast_to(row, (16, 256)), 0, 1, stride=1, stride_axis=0)


def build_stamp_bands(cols_ref, rows_ref, sc_ref, sr_ref):
    def one(k, carry):
        col, row = toeplitz(cols_ref, k), toeplitz(rows_ref, k)
        for s in range(4):
            for g in range(2):
                shift = 64 * s + 16 * g
                value = col if shift == 0 else pltpu.roll(col, shift, 1)
                sc_ref[k, 32 * s + 16 * g : 32 * s + 16 * g + 16, :] = value.astype(BF16)
        for h in range(2):
            for g in range(2):
                value = pltpu.roll(row, 64 * h + 16 * g + 6, 1)[:, :128]
                sr_ref[k, 32 * h + 16 * g : 32 * h + 16 * g + 16, :] = value.astype(BF16)
        return carry

    lax.fori_loop(0, NK, one, 0)


def build_full_bands(cols_ref, rows_ref, fc_ref, fr_ref):
    def one(k, carry):
        col, row = toeplitz(cols_ref, k), toeplitz(rows_ref, k)
        for g in range(8):
            fc_ref[k, 16 * g : 16 * g + 16, :] = pltpu.roll(col, LP - 10 + 16 * g, 1).astype(BF16)
            fr_ref[k, 16 * g : 16 * g + 16, :] = pltpu.roll(row, 6 + 16 * g, 1).astype(BF16)
        return carry

    lax.fori_loop(0, NK, one, 0)


def prepare_stamps(
    first_row, total_rows, corner_ref, count_ref, science_ref,
    pick_rows_ref, pick_columns_ref, field_ref, poly_ref, target_ref,
):
    height, width = science_ref.shape
    full = pick_columns_ref.shape[1]
    live = jnp.zeros((64, 128), F32)
    rows = jnp.zeros((64, 128), jnp.int32)
    columns = jnp.zeros((64, 128), jnp.int32)
    group = iota((1, 128), 1) // 32
    half_of = iota((64, 128), 0) // 32
    lag = iota((64, height + 2 * RP), 1) - iota((64, height + 2 * RP), 0)
    short = iota((32, height), 1) - iota((32, height), 0)
    left = iota((full, 128), 0) - iota((full, 128), 1) % 64 - (LP - 10)
    side = iota((full, 128), 1) // 64
    near = iota((width, 128), 0) - iota((width, 128), 1) % 32
    value = science_ref[...]
    parts = []
    for part in range(3):
        parts.append(value.astype(BF16))
        value = value - parts[-1].astype(F32)
    picks = []
    for slot in range(8):
        a = corner_ref[slot, 0]
        e = corner_ref[slot, 1]
        picks.append((short == a).astype(F32))
        pick_rows_ref[64 * slot : 64 * slot + 64, :] = (lag == a).astype(F32).astype(BF16)
        pick_columns_ref[slot] = ((left == e) & (side == slot % 2)).astype(F32).astype(BF16)
        here = (half_of == slot // 4) & (group == slot % 4)
        live = jnp.where(here, (slot < count_ref[0]).astype(F32), live)
        rows = jnp.where(here, a, rows)
        columns = jnp.where(here, e, columns)
    picks = jnp.concatenate(picks, axis=0).astype(BF16)
    picked = jnp.dot(picks, jnp.concatenate(parts, axis=1), preferred_element_type=F32).astype(BF16)
    for h in range(2):
        total = jnp.zeros((96, 128), F32)
        for s in range(4):
            slot = h * 4 + s
            stack = jnp.concatenate(
                [
                    picked[32 * slot : 32 * slot + 32, width * part : width * part + width]
                    for part in range(3)
                ],
                axis=0,
            )
            chosen = ((near == corner_ref[slot, 1]) & (group == s)).astype(F32).astype(BF16)
            total = total + jnp.dot(stack, chosen, preferred_element_type=F32)
        for part in range(3):
            at = slice(32 * h, 32 * h + 32)
            target_ref[part, at, :] = total[32 * part : 32 * part + 32] * live[at]
    for part in range(3, 16):
        target_ref[part] = jnp.zeros((64, 128), F32)
    rows = rows + iota((64, 128), 0) % 32 + first_row
    columns = columns + iota((64, 128), 1) % 32
    y = (2 * rows + 1).astype(F32) / total_rows - 1.0
    x = (2 * columns + 1).astype(F32) / width - 1.0
    poly_ref[0] = jnp.ones_like(x)
    poly_ref[1] = x
    poly_ref[2] = y
    poly_ref[3] = 1.5 * x * x - 0.5
    poly_ref[4] = x * y
    poly_ref[5] = 1.5 * y * y - 0.5
    field_ref[NK] = live
    for k in range(NK + 1, KP):
        field_ref[k] = jnp.zeros((64, 128), F32)


def stamp_gram(
    ext_ref, pick_rows_ref, pick_columns_ref, sc_ref, sr_ref,
    x2_ref, field_ref, poly_ref, target_ref, gram_ref,
):
    picked = jnp.dot(pick_rows_ref[...], ext_ref[...], preferred_element_type=F32).astype(BF16)
    for pair in range(4):
        window = sum(
            jnp.dot(
                picked[64 * slot : 64 * slot + 64], pick_columns_ref[slot],
                preferred_element_type=F32,
            )
            for slot in (2 * pair, 2 * pair + 1)
        )
        at = 128 * (pair % 2)
        x2_ref[64 * (pair // 2) : 64 * (pair // 2) + 64, at : at + 128] = window.astype(BF16)
    live = field_ref[NK]

    def convolve(k, carry):
        across = lax.dot_general(x2_ref[...], sc_ref[k], NT, preferred_element_type=F32)
        down = jnp.dot(sr_ref[k], across.astype(BF16), preferred_element_type=F32)
        field_ref[k] = down.astype(BF16).astype(F32) * live
        return carry

    lax.fori_loop(0, NK, convolve, 0)
    gram_ref[...] = jnp.zeros_like(gram_ref)

    def row_features(q):
        field = field_ref[:, q, :]
        parts = [field]
        for p in range(1, 6):
            parts.append(field * poly_ref[p, pl.ds(q, 1), :])
        parts.append(target_ref[:, q, :])
        return jnp.concatenate(parts, axis=0).astype(BF16)

    def add(step, carry):
        both = jnp.concatenate([row_features(2 * step), row_features(2 * step + 1)], axis=1)
        gram_ref[:, :NG] += lax.dot_general(both, both, NT, preferred_element_type=F32)
        return carry

    lax.fori_loop(0, 32, add, 0)


def full_convolution(ext_ref, fc_ref, fr_ref, across_ref, conv_ref, first, last):
    tiles = conv_ref.shape[2] // 128
    halves = conv_ref.shape[1] // 128

    def one(k, carry):
        for t in range(tiles):
            across_ref[:, 128 * t : 128 * t + 128] = lax.dot_general(
                ext_ref[:, 128 * t : 128 * t + 256], fc_ref[k], NT, preferred_element_type=F32
            ).astype(BF16)
        for t in range(halves):
            conv_ref[k, 128 * t : 128 * t + 128, :] = jnp.dot(
                fr_ref[k, :, :160],
                across_ref[128 * t : 128 * t + 160, :],
                preferred_element_type=F32,
            ).astype(BF16)
        return carry

    lax.fori_loop(first, last, one, 0)


def solve(sum_ref, prior_ref, system_ref, answer_ref, solution_ref):
    at = iota((NF, 256), 0)
    lane = iota((NF, 256), 1)
    left = sum_ref[: NG // 8].reshape(NG, 128)
    corner = sum_ref[NG // 8 :].reshape(NG - 128, 128)
    edge = jnp.concatenate([left[128:], jnp.zeros((256 - NG, 128), F32)], axis=0)
    right = jnp.concatenate([edge.T, corner[: NF - 128]], axis=0)
    wide = jnp.concatenate([left[:NF], right], axis=1)
    pixels = left[NK : NK + 1, NK : NK + 1]
    order = (at % KP) * 6 + at // KP
    used = at % KP <= NK
    right = jnp.sum(jnp.where((lane >= NF) & (lane < NF + 3), wide, 0.0), axis=1, keepdims=True)
    prior = jnp.sum(
        jnp.where((lane == order) & used, prior_ref[...], 0.0), axis=1, keepdims=True
    )
    right = right / pixels + prior
    body = jnp.where(used & (lane % KP <= NK) & (lane < NF), wide / pixels, 0.0)
    body = body + (at == lane).astype(F32)
    system_ref[...] = jnp.where((lane == NF) & used, right, body)

    def eliminate(j, carry):
        matrix = system_ref[...]
        row = system_ref[pl.ds(j, 1), :]
        column = jnp.sum(jnp.where(lane == j, matrix, 0.0), axis=1, keepdims=True)
        pivot = jnp.sum(jnp.where(lane[:1] == j, row, 0.0), axis=1, keepdims=True)
        factor = jnp.where(at[:, :1] == j, 0.0, column / pivot)
        system_ref[...] = matrix - factor * row
        return carry

    lax.fori_loop(0, NF, eliminate, 0)
    matrix = system_ref[...]
    top = jnp.sum(jnp.where(lane == NF, matrix, 0.0), axis=1, keepdims=True)
    diagonal = jnp.sum(jnp.where(lane == at, matrix, 0.0), axis=1, keepdims=True)
    answer = top / diagonal
    answer_ref[...] = jnp.broadcast_to(answer, (NF, 128))
    solution_ref[...] = jnp.sum(
        jnp.where((lane == order) & used, answer, 0.0), axis=0, keepdims=True
    )


def subtract(
    first_row, total_rows, science_ref, conv_ref, answer_ref, difference_ref,
):
    height, width = science_ref.shape
    x = (2 * iota((1, width), 1) + 1).astype(F32) / width - 1.0
    x2 = 1.5 * x * x - 0.5

    def band(step, carry):
        start = pl.multiple_of(step * 16, 16)
        y = (2 * (first_row + start + iota((16, 128), 0)) + 1).astype(F32) / total_rows - 1.0
        y2 = 1.5 * y * y - 0.5

        def term(k):
            c = [answer_ref[p * KP + k : p * KP + k + 1, :] for p in range(6)]
            flat, slope, curve = c[0] + c[2] * y + c[5] * y2, c[1] + c[4] * y, c[3]
            spread = lambda v: jnp.concatenate([v] * (width // 128), axis=1)
            return spread(flat), spread(slope), spread(curve)

        flat, slope, curve = term(NK)
        curve = jnp.broadcast_to(curve, flat.shape)
        for k in range(NK):
            value = conv_ref[k, pl.ds(start, 16), :].astype(F32)
            f, s, c = term(k)
            flat, slope, curve = flat + value * f, slope + value * s, curve + value * c
        matched = flat + slope * x + curve * x2
        difference_ref[pl.ds(start, 16), :] = science_ref[pl.ds(start, 16), :] - matched
        return carry

    lax.fori_loop(0, height // 16, band, 0)


def stamp_residuals(answer_ref, field_ref, poly_ref, target_ref, piece_ref, residual_ref):
    value = target_ref[0] + target_ref[1] + target_ref[2]
    for k in range(NK + 1):
        weight = answer_ref[k : k + 1, :]
        for p in range(1, 6):
            weight = weight + answer_ref[p * KP + k : p * KP + k + 1, :] * poly_ref[p]
        value = value - field_ref[k] * weight
    group = iota((8, 128), 1) // 32
    for slot in range(8):
        s = slot % 4
        piece = value[32 * (slot // 4) : 32 * (slot // 4) + 32]
        piece_ref[...] = pltpu.roll(piece, 128 - 32 * s, 1) if s else piece
        result = jnp.zeros((8, 128), F32)
        for m in range(4):
            part = piece_ref[pl.ds(m, 8, stride=4), :]
            part = pltpu.roll(part, 32 * m, 1) if m else part
            result = jnp.where(group == m, part, result)
        residual_ref[slot] = result


MESH = pl.DeviceIdType.MESH
TILES = NG // 8 + (NG - 128) // 8


def coords(device):
    return (device // lax.axis_size("strip"), lax.rem(device, lax.axis_size("strip")))


def send(src, dst, send_sem, recv_sem, device):
    pltpu.make_async_remote_copy(
        src_ref=src, dst_ref=dst, send_sem=send_sem, recv_sem=recv_sem,
        device_id=coords(device), device_id_type=MESH,
    ).start()


def await_bytes(ref, sem):
    pltpu.make_async_copy(ref, ref, sem).wait()


def pack(total, blocks_ref, route_ref, offset_ref, out_ref, spot_ref):
    count = route_ref.shape[0]
    height = blocks_ref.shape[0] // count
    goal = route_ref[...].astype(F32)
    down, along = iota((count, count), 0), iota((count, count), 1)
    goal_row = jnp.sum(jnp.where(down == along, goal, 0.0), axis=0, keepdims=True)
    same = goal == goal_row
    rank = jnp.sum(jnp.where(same & (along < down), 1.0, 0.0), axis=1, keepdims=True)
    rank_row = jnp.sum(jnp.where(same & (down < along), 1.0, 0.0), axis=0, keepdims=True)
    span = 2 * height * count
    column = iota((1, span), 1)
    owner = lax.rem(column, height * count) // height
    code = jnp.sum(
        jnp.where(iota((count, span), 0) == owner, goal * 16.0 + rank * 4.0, 0.0),
        axis=0, keepdims=True,
    ).astype(jnp.int32)
    code = code + column // (height * count) * 8 + lax.rem(column, height)
    source = jnp.concatenate([blocks_ref[:, :256], blocks_ref[:, 256:]], axis=0)

    def chunk(step, carry):
        pick = (iota((512, span), 0) + step * 512 == code).astype(F32).astype(BF16)
        rows = jnp.dot(pick, source, preferred_element_type=F32).astype(BF16)
        out_ref[pl.ds(step * 32, 32)] = rows.reshape(32, 16, 256)
        return carry

    lax.fori_loop(0, total // 32, chunk, 0)
    slot_row = goal_row * 2.0 + rank_row
    offset_row = offset_ref[...].astype(F32)
    wanted = (2 * iota((total, count), 0)).astype(F32)
    first, second = [
        jnp.sum(jnp.where(wanted + r == slot_row, offset_row, 0.0), axis=1, keepdims=True)
        for r in (0.0, 1.0)
    ]
    lane = iota((total, 128), 1)
    spots = jnp.where(lane % 8 < 4, first, second) + (lane % 4).astype(F32)
    spot_ref[:, 0, :] = spots


def place_blocks(total, in_ref, spot_ref, frame_rows):
    span = total * 16
    spots = jnp.concatenate([spot_ref[:, 0, :]] * (span // 128), axis=1)
    column = iota((total, span), 1)
    spot = jnp.sum(jnp.where(column // 16 == iota((total, span), 0), spots, 0.0), axis=0, keepdims=True)
    spot = spot.astype(jnp.int32)
    lands = iota((frame_rows, span), 0) == spot
    upper = iota((1, span), 1) // 8 % 2
    rows = in_ref[...].reshape(span, 256)
    halves = [
        jnp.dot((lands & (upper == h)).astype(F32).astype(BF16), rows, preferred_element_type=F32)
        for h in range(2)
    ]
    return jnp.concatenate(halves, axis=1).astype(BF16)


def whole_kernel(
    total, corner_ref, count_ref, blocks_ref, route_ref, offset_ref, warp_ref, science_ref,
    cols_ref, rows_ref, prior_ref,
    difference_ref, residual_ref, solution_ref,
    out_ref, in_ref, spot_out_ref, spot_in_ref, edge_ref, ext_ref, pick_rows_ref, pick_columns_ref,
    sc_ref, sr_ref, x2_ref, field_ref, poly_ref, target_ref, gram_ref,
    tile_ref, part_ref, own_ref, sum_ref,
    fc_ref, fr_ref, across_ref, conv_ref, system_ref, answer_ref, piece_ref,
    block_sems, spot_sems, up_sems, down_sems, part_sems, sum_sems,
):
    me = lax.axis_index("ccd") * lax.axis_size("strip") + lax.axis_index("strip")
    height = science_ref.shape[0]
    barrier = pltpu.get_barrier_semaphore()

    def greet(step, carry):
        peer = lax.rem(me + step, total)
        pl.semaphore_signal(barrier, inc=1, device_id=coords(peer), device_id_type=MESH)
        return carry

    lax.fori_loop(1, total, greet, 0)
    pack(total, blocks_ref, route_ref, offset_ref, out_ref, spot_out_ref)
    in_ref[me] = out_ref[me]
    spot_in_ref[me] = spot_out_ref[me]
    pl.semaphore_wait(barrier, total - 1)

    def deliver(step, carry):
        peer = lax.rem(me + step, total)
        send(spot_out_ref.at[peer], spot_in_ref.at[me], spot_sems.at[0], spot_sems.at[1], peer)
        send(out_ref.at[peer], in_ref.at[me], block_sems.at[0], block_sems.at[1], peer)
        return carry

    lax.fori_loop(1, total, deliver, 0)
    first_row, total_rows = me * height, total * height
    prepare_stamps(
        first_row, total_rows, corner_ref, count_ref, science_ref,
        pick_rows_ref, pick_columns_ref, field_ref, poly_ref, target_ref,
    )
    build_stamp_bands(cols_ref, rows_ref, sc_ref, sr_ref)
    build_full_bands(cols_ref, rows_ref, fc_ref, fr_ref)
    most = pl.ds(0, total - 1)
    await_bytes(spot_in_ref.at[most], spot_sems.at[1])
    await_bytes(in_ref.at[most], block_sems.at[1])
    frame = place_blocks(total, in_ref, spot_in_ref, warp_ref.shape[1])
    template = jnp.dot(warp_ref[...], frame, preferred_element_type=F32).astype(BF16).astype(F32)
    template = jnp.concatenate([template, jnp.zeros((height, 2 * LP), F32)], axis=1)
    template = pltpu.roll(template, LP, 1)
    ext_ref[RP : RP + height, :] = template.astype(BF16)

    @pl.when(me < total - 1)
    def _():
        send(ext_ref.at[pl.ds(height, RP)], edge_ref.at[0], up_sems.at[0], up_sems.at[1], me + 1)

    @pl.when(me > 0)
    def _():
        send(ext_ref.at[pl.ds(RP, RP)], edge_ref.at[1], down_sems.at[0], down_sems.at[1], me - 1)

    await_bytes(spot_out_ref.at[most], spot_sems.at[0])
    await_bytes(out_ref.at[most], block_sems.at[0])
    blank = jnp.zeros((RP, ext_ref.shape[1]), F32)
    ext_ref[:RP, :] = blank.astype(BF16)
    ext_ref[RP + height :, :] = blank.astype(BF16)

    @pl.when(me > 0)
    def _():
        await_bytes(edge_ref.at[0], up_sems.at[1])
        ext_ref[:RP, :] = edge_ref[0]
        await_bytes(edge_ref.at[1], down_sems.at[0])

    @pl.when(me < total - 1)
    def _():
        await_bytes(edge_ref.at[1], down_sems.at[1])
        ext_ref[RP + height :, :] = edge_ref[1]
        await_bytes(edge_ref.at[0], up_sems.at[0])

    stamp_gram(
        ext_ref, pick_rows_ref, pick_columns_ref, sc_ref, sr_ref,
        x2_ref, field_ref, poly_ref, target_ref, gram_ref,
    )
    for t in range(NG // 8):
        tile_ref[t] = gram_ref[8 * t : 8 * t + 8, :128]
    for t in range(NG // 8, TILES):
        at = 128 + 8 * (t - NG // 8)
        tile_ref[t] = gram_ref[at : at + 8, 128:]

    def give(step, carry):
        t = lax.rem(me + step, TILES)

        @pl.when(t != me)
        def _():
            send(tile_ref.at[t], part_ref.at[me], part_sems.at[0], part_sems.at[1], t)

        return carry

    lax.fori_loop(0, TILES, give, 0)
    full_convolution(ext_ref, fc_ref, fr_ref, across_ref, conv_ref, 0, NK // 2)

    @pl.when(me < TILES)
    def _():
        part_ref[me] = tile_ref[me]
        await_bytes(part_ref.at[most], part_sems.at[1])
        own_ref[...] = jnp.sum(part_ref[...], axis=0)
        sum_ref[me] = own_ref[...]

        def spread(step, carry):
            peer = lax.rem(me + step, total)
            send(own_ref, sum_ref.at[me], sum_sems.at[0], sum_sems.at[1], peer)
            return carry

        lax.fori_loop(1, total, spread, 0)

    full_convolution(ext_ref, fc_ref, fr_ref, across_ref, conv_ref, NK // 2, NK)

    @pl.when(me < TILES)
    def _():
        await_bytes(sum_ref.at[pl.ds(0, TILES - 1)], sum_sems.at[1])
        await_bytes(tile_ref.at[pl.ds(0, TILES - 1)], part_sems.at[0])
        await_bytes(part_ref.at[most], sum_sems.at[0])

    @pl.when(me >= TILES)
    def _():
        await_bytes(sum_ref, sum_sems.at[1])
        await_bytes(tile_ref, part_sems.at[0])

    solve(sum_ref, prior_ref, system_ref, answer_ref, solution_ref)
    stamp_residuals(answer_ref, field_ref, poly_ref, target_ref, piece_ref, residual_ref)
    subtract(first_row, total_rows, science_ref, conv_ref, answer_ref, difference_ref)


VM = pl.BlockSpec(memory_space=pltpu.VMEM)
SM = pl.BlockSpec(memory_space=pltpu.SMEM)


STAMP_SCRATCH = [
    pltpu.VMEM((NK, 128, 256), BF16),
    pltpu.VMEM((NK, 64, 128), BF16),
    pltpu.VMEM((128, 256), BF16),
    pltpu.VMEM((KP, 64, 128), F32),
    pltpu.VMEM((8, 64, 128), F32),
    pltpu.VMEM((16, 64, 128), F32),
]


def padded_taps(taps):
    return jnp.pad(taps.astype(F32), ((0, KP - taps.shape[0]), (0, 256 - taps.shape[1])))


def local(
    coadd_blocks, block_route, block_offset, warp_matrix, science, basis_columns, basis_rows,
    stamp_corner, stamp_count, kernel_prior,
):
    total = lax.axis_size("ccd") * lax.axis_size("strip")
    height, width = science.shape
    rows, columns = height + 2 * RP, width + 2 * LP
    pair = pltpu.SemaphoreType.DMA((2,))
    prior = jnp.pad(kernel_prior[None, :], ((0, 0), (0, 256 - kernel_prior.shape[0])))
    difference, residual, answer = pl.pallas_call(
        functools.partial(whole_kernel, total),
        out_shape=(
            jax.ShapeDtypeStruct((height, width), F32),
            jax.ShapeDtypeStruct((8, 8, 128), F32),
            jax.ShapeDtypeStruct((1, 256), F32),
        ),
        in_specs=[SM, SM] + [VM] * 8,
        out_specs=(VM, VM, VM),
        scratch_shapes=[
            pltpu.VMEM((total, 16, 256), BF16),
            pltpu.VMEM((total, 16, 256), BF16),
            pltpu.VMEM((total, 1, 128), F32),
            pltpu.VMEM((total, 1, 128), F32),
            pltpu.VMEM((2, RP, columns), BF16),
            pltpu.VMEM((rows, columns), BF16),
            pltpu.VMEM((512, rows), BF16),
            pltpu.VMEM((8, columns, 128), BF16),
        ]
        + STAMP_SCRATCH
        + [
            pltpu.VMEM((NG, 256), F32),
            pltpu.VMEM((TILES, 8, 128), F32),
            pltpu.VMEM((total, 8, 128), F32),
            pltpu.VMEM((8, 128), F32),
            pltpu.VMEM((TILES, 8, 128), F32),
            pltpu.VMEM((NK, 128, 256), BF16),
            pltpu.VMEM((NK, 128, 256), BF16),
            pltpu.VMEM((rows, width), BF16),
            pltpu.VMEM((NK, height, width), BF16),
            pltpu.VMEM((NF, 256), F32),
            pltpu.VMEM((NF, 128), F32),
            pltpu.VMEM((32, 128), F32),
        ]
        + [pair] * 6,
        compiler_params=pltpu.CompilerParams(
            vmem_limit_bytes=52 << 20, collective_id=0, has_side_effects=True
        ),
    )(
        stamp_corner, stamp_count, coadd_blocks, block_route, block_offset[None, :], warp_matrix,
        science, padded_taps(basis_columns), padded_taps(basis_rows), prior,
    )
    return (
        difference,
        residual.reshape(8, SS * SS),
        answer[0, : kernel_prior.shape[0]],
    )


def solution(mesh):
    split = P(("ccd", "strip"), None)
    flat = P(("ccd", "strip"))
    in_specs = (split, split, flat, split, split, P(), P(), split, flat, P())
    out_specs = (split, split, P())
    return jax.shard_map(local, mesh=mesh, in_specs=in_specs, out_specs=out_specs, check_vma=False)
```

time: 807 us -> 75.7 us (0.09); the launches traced: 792 us -> 75.4 us
  other arithmetic: 404 us -> 0.01 us
  local copies, waits for them, and re-layouts: 110 us -> 8.21 us
  waiting for transfers between devices: 89.8 us -> 0 us
  matrix products: 66.7 us -> 0 us
  Pallas kernels: 0 us -> 65.8 us
  blocking collectives: 50.5 us -> 0 us
  loops' own time: 38.1 us -> 0 us
  starting transfers between devices: 18.8 us -> 0 us
  between operations: 15.1 us -> 1.31 us
    sub x270 -> x0, other arithmetic: 186 us -> none  [the longest x132 172 us: eliminate(): vector - factor * pivot_value]
    reduce_sum x268 -> x0, other arithmetic: 107 us -> none  [the longest x132 80.2 us: eliminate(): pivot = jnp.sum(pivot_row * marker)]
    psum x1 -> x0, waiting for transfers between devices: 79.3 us -> none  [global_fit(): lax.psum((normal_matrix, right_side, pixels), ('ccd', 'strip'))]
    dot_general x71 -> x0, matrix products: 66.7 us -> none  [the longest x32 30.8 us: fit_terms(): jnp.dot(features.astype(jnp.float32), weights * targets, precision=lax.Pr...]
    pallas_call x0 -> x1, Pallas kernels: none -> 65.8 us  [local(): pl.pallas_call(functools.partial(whole_kernel, total), out_shape=(jax.Sha...]
    while x224 -> x0, local copies, waits for them, and re-layouts: 63.3 us -> none
    add x38 -> x0, other arithmetic: 44.7 us -> none  [the longest x32 39.7 us: accumulate(): return (partial_value[0] + normal_part, partial_value[1] + right_part)]
    psum x1 -> x0, blocking collectives: 42.9 us -> none  [global_fit(): lax.psum((normal_matrix, right_side, pixels), ('ccd', 'strip'))]
  transfers between devices with their start and end apart: 5 -> 0, of which waited for: 3 -> 0; matrix products, arithmetic and copies ran while one was open for 2% -> 0% of each run, Pallas kernels for 0% -> 0%
where the time goes in v1:
time: 75.7 us; the launch traced here: 75.4 us
  Pallas kernels  65.8 us (87%)
  local copies, waits for them, and re-layouts  8.21 us (11%)
  between operations  1.31 us (2%)
    pallas_call x1, Pallas kernels, local(): pl.pallas_call(functools.partial(whole_kernel, total), out_shape=(jax.Sha...  65.8 us
    unnamed x23, local copies, waits for them, and re-layouts  8.2 us

profile of v1, /device:TPU:0, one launch (start us, length us, event | category | flops | bytes accessed | tf_op | source)
XLA Modules:
  0.0 75.4 jit_solution(10715186142549234938)
XLA Ops:
  1.3 0.0 copy-start.7
  1.3 0.7 copy-done.7
  2.0 0.0 copy-start.6
  2.0 0.7 copy-done.6
  2.6 0.0 copy-start.8
  2.6 0.1 copy.13.corner_ref
  2.7 0.6 copy-done.8
  3.3 0.0 copy-start.4
  3.3 0.0 copy-start.5
  3.3 0.1 copy.14.route_ref
  3.4 0.6 copy-done.4
  4.0 0.0 copy-done.5
  4.0 0.0 copy-start.3
  4.0 0.6 copy-done.3
  4.7 0.0 copy-start
  4.7 1.0 %copy-done = f32[256,512]{1,0:T(8,128)S(1)} copy-done((f32[256,512]{1,0:T(8,128)S(1)}, f32[256,512]{1,0:T(8,128)}, u32[]{:S(2)}) %copy-start) | copy-done | bytes 524312
  5.7 0.0 copy-start.1
  5.7 0.9 %copy-done.1 = bf16[256,384]{1,0:T(8,128)(2,1)S(1)} copy-done((bf16[256,384]{1,0:T(8,128)(2,1)S(1)}, bf16[256,384]{1,0:T(8,128)(2,1)}, u32[]{:S(2)}) %copy-start.1) | copy-done | bytes 196632
  6.6 0.0 copy-start.2
  6.6 0.9 %copy-done.2 = bf16[128,512]{1,0:T(8,128)(2,1)S(1)} copy-done((bf16[128,512]{1,0:T(8,128)(2,1)S(1)}, bf16[128,512]{1,0:T(8,128)(2,1)}, u32[]{:S(2)}) %copy-start.2) | copy-done | bytes 131096
  7.5 65.8 %shard_map.121 = (f32[256,512]{1,0:T(8,128)S(1)}, f32[8,8,128]{2,1,0:T(8,128)S(1)}, f32[1,256]{1,0:T(1,128)S(1)}) custom-call(s32[8,2]{1,0:T(8,128)S(1)} %copy.13.corner_ref, s32[1]{0:T(128)S(6)} %copy.20.count_ref, bf16[128,512]{1,0:T(8,128)(2,1)S(1)} %copy-done.2, s32[32,1]{1,0:T(8,128)S(1)} %copy.14.route_ref, s32[1,32]{1,0:T(1,128)S(1)} %bitcast.10, ...), custom_call_target="tpu_custom_call" | custom-call | tf_op jit(solution)/shard_map/pallas_call | solution.py:507
  73.4 0.6 copy.17
  74.0 0.8 %copy.21 = f32[256,512]{1,0:T(8,128)} copy(f32[256,512]{1,0:T(8,128)S(1)} %get-tuple-element.14) | data formatting | bytes 1048576
  74.8 0.6 copy.22
  (2 shorter events, 0.0 us)
Async XLA Ops:
  1.3 0.7 copy-start.7
  2.0 0.7 copy-start.6
  2.6 0.7 copy-start.8
  3.3 0.7 copy-start.4
  3.3 0.7 copy-start.5
  4.0 0.7 copy-start.3
  4.7 1.0 %copy-start = (f32[256,512]{1,0:T(8,128)S(1)}, f32[256,512]{1,0:T(8,128)}, u32[]{:S(2)}) copy-start(f32[256,512]{1,0:T(8,128)} %science_ref.1) | copy-start | bytes 1572868
  5.7 0.9 %copy-start.1 = (bf16[256,384]{1,0:T(8,128)(2,1)S(1)}, bf16[256,384]{1,0:T(8,128)(2,1)}, u32[]{:S(2)}) copy-start(bf16[256,384]{1,0:T(8,128)(2,1)} %warp_ref.1) | copy-start | bytes 589828
  6.6 0.9 %copy-start.2 = (bf16[128,512]{1,0:T(8,128)(2,1)S(1)}, bf16[128,512]{1,0:T(8,128)(2,1)}, u32[]{:S(2)}) copy-start(bf16[128,512]{1,0:T(8,128)(2,1)} %blocks_ref.1) | copy-start | bytes 393220

commit v2 on v1

--- a/solution.py
+++ b/solution.py
@@ -11,6 +11,7 @@
 NK = 21
 KP = 24
 NF = 6 * KP
+PIVOTS = 4
 NG = NF + 16
 LP = 64
 RP = 16
@@ -205,16 +206,28 @@
     body = body + (at == lane).astype(F32)
     system_ref[...] = jnp.where((lane == NF) & used, right, body)
 
-    def eliminate(j, carry):
+    def eliminate(step, carry):
+        first = pl.multiple_of(step * PIVOTS, PIVOTS)
         matrix = system_ref[...]
-        row = system_ref[pl.ds(j, 1), :]
-        column = jnp.sum(jnp.where(lane == j, matrix, 0.0), axis=1, keepdims=True)
-        pivot = jnp.sum(jnp.where(lane[:1] == j, row, 0.0), axis=1, keepdims=True)
-        factor = jnp.where(at[:, :1] == j, 0.0, column / pivot)
-        system_ref[...] = matrix - factor * row
-        return carry
-
-    lax.fori_loop(0, NF, eliminate, 0)
+        each = range(PIVOTS)
+        rows = [system_ref[pl.ds(first + i, 1), :] for i in each]
+        pick = lambda v, i: jnp.sum(
+            jnp.where(lane[: v.shape[0]] == first + i, v, 0.0), axis=1, keepdims=True
+        )
+        columns = [pick(matrix, i) for i in each]
+        heads = [[pick(rows[i], m) for m in each] for i in each]
+        for i in each:
+            factor = jnp.where(at[:, :1] == first + i, 0.0, columns[i] / heads[i][i])
+            matrix = matrix - factor * rows[i]
+            for m in range(i + 1, PIVOTS):
+                columns[m] = columns[m] - factor * heads[i][m]
+                scale = heads[m][i] / heads[i][i]
+                rows[m] = rows[m] - scale * rows[i]
+                heads[m] = [heads[m][n] - scale * heads[i][n] for n in each]
+        system_ref[...] = matrix
+        return carry
+
+    lax.fori_loop(0, NF // PIVOTS, eliminate, 0)
     matrix = system_ref[...]
     top = jnp.sum(jnp.where(lane == NF, matrix, 0.0), axis=1, keepdims=True)
     diagonal = jnp.sum(jnp.where(lane == at, matrix, 0.0), axis=1, keepdims=True)

time: 75.7 us -> 67.5 us (0.89)
  Pallas kernels: 65.8 us -> 57.7 us
    pallas_call x1, Pallas kernels: 65.8 us -> 57.7 us  [local(): pl.pallas_call(functools.partial(whole_kernel, total), out_shape=(jax.Sha...]
where the time goes in v2:
time: 67.5 us; the launch traced here: 67.2 us
  Pallas kernels  57.7 us (85%)
  local copies, waits for them, and re-layouts  8.21 us (12%)
  between operations  1.31 us (2%)
    pallas_call x1, Pallas kernels, local(): pl.pallas_call(functools.partial(whole_kernel, total), out_shape=(jax.Sha...  57.7 us
    unnamed x23, local copies, waits for them, and re-layouts  8.2 us

profile of v2, /device:TPU:0, one launch (start us, length us, event | category | flops | bytes accessed | tf_op | source)
XLA Modules:
  0.0 67.2 jit_solution(12541345574046018915)
XLA Ops:
  1.3 0.0 copy-start.7
  1.3 0.7 copy-done.7
  2.0 0.0 copy-start.6
  2.0 0.7 copy-done.6
  2.6 0.0 copy-start.8
  2.6 0.1 copy.13.corner_ref
  2.7 0.6 copy-done.8
  3.3 0.0 copy-start.4
  3.3 0.0 copy-start.5
  3.3 0.1 copy.14.route_ref
  3.4 0.6 copy-done.4
  4.0 0.0 copy-done.5
  4.0 0.0 copy-start.3
  4.0 0.6 copy-done.3
  4.7 0.0 copy-start
  4.7 1.0 %copy-done = f32[256,512]{1,0:T(8,128)S(1)} copy-done((f32[256,512]{1,0:T(8,128)S(1)}, f32[256,512]{1,0:T(8,128)}, u32[]{:S(2)}) %copy-start) | copy-done | bytes 524312
  5.7 0.0 copy-start.1
  5.7 0.9 %copy-done.1 = bf16[256,384]{1,0:T(8,128)(2,1)S(1)} copy-done((bf16[256,384]{1,0:T(8,128)(2,1)S(1)}, bf16[256,384]{1,0:T(8,128)(2,1)}, u32[]{:S(2)}) %copy-start.1) | copy-done | bytes 196632
  6.6 0.0 copy-start.2
  6.6 0.9 %copy-done.2 = bf16[128,512]{1,0:T(8,128)(2,1)S(1)} copy-done((bf16[128,512]{1,0:T(8,128)(2,1)S(1)}, bf16[128,512]{1,0:T(8,128)(2,1)}, u32[]{:S(2)}) %copy-start.2) | copy-done | bytes 131096
  7.5 57.7 %shard_map.121 = (f32[256,512]{1,0:T(8,128)S(1)}, f32[8,8,128]{2,1,0:T(8,128)S(1)}, f32[1,256]{1,0:T(1,128)S(1)}) custom-call(s32[8,2]{1,0:T(8,128)S(1)} %copy.13.corner_ref, s32[1]{0:T(128)S(6)} %copy.20.count_ref, bf16[128,512]{1,0:T(8,128)(2,1)S(1)} %copy-done.2, s32[32,1]{1,0:T(8,128)S(1)} %copy.14.route_ref, s32[1,32]{1,0:T(1,128)S(1)} %bitcast.10, ...), custom_call_target="tpu_custom_call" | custom-call | tf_op jit(solution)/shard_map/pallas_call | solution.py:520
  65.2 0.6 copy.17
  65.8 0.8 %copy.21 = f32[256,512]{1,0:T(8,128)} copy(f32[256,512]{1,0:T(8,128)S(1)} %get-tuple-element.14) | data formatting | bytes 1048576
  66.6 0.6 copy.22
  (2 shorter events, 0.0 us)
Async XLA Ops:
  1.3 0.7 %copy-start.7 = (f32[132]{0:T(256)S(1)}, f32[132]{0:T(256)}, u32[]{:S(2)}) copy-start(f32[132]{0:T(256)} %param.19) | copy-start | bytes 1588
  2.0 0.7 %copy-start.6 = (s32[8,2]{0,1:T(2,128)S(1)}, s32[8,2]{0,1:T(2,128)}, u32[]{:S(2)}) copy-start(s32[8,2]{0,1:T(2,128)} %param.17) | copy-start | bytes 196
  2.6 0.7 copy-start.8
  3.3 0.7 %copy-start.4 = (bf16[21,21]{1,0:T(8,128)(2,1)S(1)}, bf16[21,21]{1,0:T(8,128)(2,1)}, u32[]{:S(2)}) copy-start(bf16[21,21]{1,0:T(8,128)(2,1)} %param.16) | copy-start | bytes 2650
  3.3 0.7 %copy-start.5 = (bf16[21,21]{1,0:T(8,128)(2,1)S(1)}, bf16[21,21]{1,0:T(8,128)(2,1)}, u32[]{:S(2)}) copy-start(bf16[21,21]{1,0:T(8,128)(2,1)} %param.15) | copy-start | bytes 2650
  4.0 0.7 copy-start.3
  4.7 1.0 %copy-start = (f32[256,512]{1,0:T(8,128)S(1)}, f32[256,512]{1,0:T(8,128)}, u32[]{:S(2)}) copy-start(f32[256,512]{1,0:T(8,128)} %science_ref.1) | copy-start | bytes 1572868
  5.7 0.9 %copy-start.1 = (bf16[256,384]{1,0:T(8,128)(2,1)S(1)}, bf16[256,384]{1,0:T(8,128)(2,1)}, u32[]{:S(2)}) copy-start(bf16[256,384]{1,0:T(8,128)(2,1)} %warp_ref.1) | copy-start | bytes 589828
  6.6 0.9 %copy-start.2 = (bf16[128,512]{1,0:T(8,128)(2,1)S(1)}, bf16[128,512]{1,0:T(8,128)(2,1)}, u32[]{:S(2)}) copy-start(bf16[128,512]{1,0:T(8,128)(2,1)} %blocks_ref.1) | copy-start | bytes 393220
